TPU v7x, 32 devices: a whole 2x2x4 slice. The times are simulated.
32 devices in a mesh: row: 4 (over x, core), col: 8 (over z, y).
Axes of the slice: x: 2, y: 2, z: 4, core: 2. Of those that a mesh axis runs over, the one named last changes fastest.
Arguments:
- matrix: float32 [8192, 16384], P('row', 'col'), may hold values from -40 to 40
Outputs:
- r_rows: float32 [512, 16384], P(None, 'col')
- scaled_basis: float32 [8192, 512], P('row')
- trailing: float32 [8192, 16384], P('row', 'col')
All inputs are finite; a program needn't handle non-finite values.
Results may differ from a plain program's by a relative error of at most 0.00013.
Values sent between devices are 32-bit elements; how exact they have to be, the bound alone decides.
A program may use at most 128 MiB of HBM per device.

v0:
```python
import math

import jax
import jax.numpy as jnp
from jax import lax
from jax.sharding import PartitionSpec as P

B = 256
PANELS = 2


def spread(shard, axis, root):
    mine = lax.axis_index(axis) == root
    return lax.psum(jnp.where(mine, shard, jnp.zeros_like(shard)), axis)


def product(left, right):
    return jnp.dot(left, right, precision=lax.Precision.HIGHEST)


def on_device(matrix):
    current = matrix
    total_rows = matrix.shape[0] * lax.axis_size("row")
    root_rows = math.sqrt(total_rows)
    r_blocks = []
    basis_blocks = []
    for panel_index in range(PANELS):
        panel_cols = spread(current[:, :B], "col", panel_index)
        gram_matrix, cross_terms = lax.psum(
            (product(panel_cols.T, panel_cols), product(panel_cols.T, current)), "row"
        )
        lower_factor = jnp.linalg.cholesky(gram_matrix)
        orthonormal = jax.scipy.linalg.solve_triangular(lower_factor, panel_cols.T, lower=True).T
        coupling = jax.scipy.linalg.solve_triangular(lower_factor, cross_terms, lower=True)
        current = current - product(orthonormal, coupling)
        r_blocks.append(coupling)
        basis_blocks.append(orthonormal * root_rows)
    return (jnp.concatenate(r_blocks, axis=0), jnp.concatenate(basis_blocks, axis=1), current)


def solution(mesh):
    placed = (P("row", "col"),)
    return jax.shard_map(
        on_device,
        mesh=mesh,
        in_specs=placed,
        out_specs=(P(None, "col"), P("row", None), P("row", "col")),
        check_vma=False,
    )
```

profile of v0, /device:TPU:29, one launch (start us, length us, event | category | flops | bytes accessed | tf_op | source)
XLA Modules:
  0.0 574.8 jit_solution(9748706019141309033)
XLA Ops:
  7.2 3.0 slice_select_fusion.1
  10.3 103.5 %all-reduce.8.cloned.1.call-done = f32[2048,256]{1,0:T(8,128)} async-done(((f32[2048,256]{1,0:T(8,128)}), f32[2048,256]{1,0:T(8,128)}) %all-reduce.8.cloned.1.call-update) | async-done | bytes 2097168 | tf_op jit(solution)/shard_map/psum | solution.py:14
  113.8 6.5 %fusion.34 = f32[256,256]{0,1:T(8,128)} fusion(f32[2048,256]{1,0:T(8,128)} %all-reduce.8.cloned.1.call-done), kind=kOutput, calls=%fused_computation.80 | convolution fusion | flops 1610612736 | bytes 2359296 | tf_op jit(solution)/shard_map/dot_general | solution.py:18
  120.3 17.7 %fusion.35 = f32[256,2048]{1,0:T(8,128)} fusion(f32[2048,256]{1,0:T(8,128)S(1)} %copy-done, f32[2048,2048]{1,0:T(8,128)} %param.4), kind=kOutput, calls=%fused_computation.81 | convolution fusion | flops 12884901888 | bytes 20971520 | tf_op jit(solution)/shard_map/dot_general | solution.py:18
  138.3 56.5 %all-reduce.14.cloned.1.call-done = (f32[256,2048]{1,0:T(8,128)}, f32[256,256]{0,1:T(8,128)}) async-done(((f32[256,2048]{1,0:T(8,128)}, f32[256,256]{0,1:T(8,128)}), (f32[256,2048]{1,0:T(8,128)}, f32[256,256]{0,1:T(8,128)})) %all-reduce.14.cloned.1.call-update) | async-done | bytes 2359312 | tf_op jit(solution)/shard_map/psum | solution.py:29
  194.8 1.1 copy.5
  195.9 1.0 fusion.15
  196.9 11.7 %cholesky.130 = f32[128,128]{1,0:T(8,128)S(1)} custom-call(f32[128,128]{1,0:T(8,128)S(1)} %cholesky.194), custom_call_target="Cholesky" | custom-call | tf_op jit(solution)/shard_map/jit(cholesky)/cholesky | solution.py:32
  208.6 9.8 %custom-call.15 = f32[1,128,128]{1,2,0:T(8,128)S(1)} custom-call(f32[1,128,128]{2,1,0:T(8,128)S(1)} %get-tuple-element.69), custom_call_target="InvertDiagBlocksLowerTriangular" | custom-call | tf_op jit(solution)/shard_map/jit(cholesky)/cholesky | solution.py:32
  219.0 11.7 %cholesky.147 = f32[128,128]{1,0:T(8,128)S(1)} custom-call(f32[128,128]{1,0:T(8,128)S(1)} %convolution_subtract_fusion.7), custom_call_target="Cholesky" | custom-call | tf_op jit(solution)/shard_map/jit(cholesky)/cholesky | solution.py:32
  230.7 0.6 compare_reduce_fusion.2
  232.8 4.4 while.8
  233.8 1.4 bitcast_dynamic-update-slice_fusion.4
  235.8 1.4 bitcast_dynamic-update-slice_fusion.4
  237.2 19.7 %custom-call.16 = f32[2,128,128]{1,2,0:T(8,128)S(1)} custom-call(f32[2,128,128]{2,1,0:T(8,128)S(1)} %get-tuple-element.31), custom_call_target="InvertDiagBlocksLowerTriangular" | custom-call | tf_op jit(solution)/shard_map/jit(_solve_triangular)/triangular_solve | solution.py:34
  256.9 1.1 fusion.10
  258.0 1.8 convolution_subtract_fusion.4
  259.8 1.1 fusion.22
  260.9 1.1 fusion.12
  261.9 1.0 convolution_subtract_fusion.5
  263.0 1.1 fusion.23
  264.1 18.9 %convolution_subtract_fusion.1 = f32[2048,2048]{1,0:T(8,128)} fusion(f32[2048,2048]{1,0:T(8,128)} %param.4, f32[128,2048]{1,0:T(8,128)S(1)} %fusion.23, f32[128,2048]{1,0:T(8,128)S(1)} %fusion.12, f32[128,2048]{1,0:T(8,128)S(1)} %fusion.22, f32[128,2048]{1,0:T(8,128)S(1)} %fusion.10), kind=kOutput, calls=%fused_computation.5 | convolution fusion | flops 12890144768 | bytes 37748736 | tf_op jit(solution)/shard_map/dot_general | solution.py:18
  283.0 3.0 slice_select_fusion
  286.1 101.0 %all-reduce.10.cloned.1.call-done = f32[2048,256]{1,0:T(8,128)} async-done(((f32[2048,256]{1,0:T(8,128)}), f32[2048,256]{1,0:T(8,128)}) %all-reduce.10.cloned.1.call-update) | async-done | bytes 2097168 | tf_op jit(solution)/shard_map/psum | solution.py:14
  387.1 6.5 %fusion.36 = f32[256,256]{0,1:T(8,128)} fusion(f32[2048,256]{1,0:T(8,128)} %all-reduce.10.cloned.1.call-done), kind=kOutput, calls=%fused_computation.82 | convolution fusion | flops 1610612736 | bytes 2359296 | tf_op jit(solution)/shard_map/dot_general | solution.py:18
  393.6 17.9 %fusion.37 = f32[256,2048]{1,0:T(8,128)} fusion(f32[2048,256]{1,0:T(8,128)S(1)} %copy-done.1, f32[2048,2048]{1,0:T(8,128)} %convolution_subtract_fusion.1), kind=kOutput, calls=%fused_computation.83 | convolution fusion | flops 12884901888 | bytes 20971520 | tf_op jit(solution)/shard_map/dot_general | solution.py:18
  411.5 2.9 multiply_bitcast_fusion.1
  414.4 53.9 %all-reduce.12.cloned.1.call-done = (f32[256,2048]{1,0:T(8,128)}, f32[256,256]{0,1:T(8,128)}) async-done(((f32[256,2048]{1,0:T(8,128)}, f32[256,256]{0,1:T(8,128)}), (f32[256,2048]{1,0:T(8,128)}, f32[256,256]{0,1:T(8,128)})) %all-reduce.12.cloned.1.call-update) | async-done | bytes 2359312 | tf_op jit(solution)/shard_map/psum | solution.py:29
  468.3 1.1 copy.7
  469.3 1.0 fusion.14
  470.4 11.7 %cholesky.164 = f32[128,128]{1,0:T(8,128)S(1)} custom-call(f32[128,128]{1,0:T(8,128)S(1)} %cholesky.197), custom_call_target="Cholesky" | custom-call | tf_op jit(solution)/shard_map/jit(cholesky)/cholesky | solution.py:32
  482.7 9.8 %custom-call.18 = f32[1,128,128]{1,2,0:T(8,128)S(1)} custom-call(f32[1,128,128]{2,1,0:T(8,128)S(1)} %get-tuple-element.65), custom_call_target="InvertDiagBlocksLowerTriangular" | custom-call | tf_op jit(solution)/shard_map/jit(cholesky)/cholesky | solution.py:32
  493.1 11.7 %cholesky.181 = f32[128,128]{1,0:T(8,128)S(1)} custom-call(f32[128,128]{1,0:T(8,128)S(1)} %convolution_subtract_fusion.6), custom_call_target="Cholesky" | custom-call | tf_op jit(solution)/shard_map/jit(cholesky)/cholesky | solution.py:32
  504.8 0.7 compare_reduce_fusion
  506.9 4.1 while.9
  507.5 1.4 bitcast_dynamic-update-slice_fusion.5
  509.6 1.4 bitcast_dynamic-update-slice_fusion.5
  511.0 19.9 %custom-call.19 = f32[2,128,128]{1,2,0:T(8,128)S(1)} custom-call(f32[2,128,128]{2,1,0:T(8,128)S(1)} %get-tuple-element.33), custom_call_target="InvertDiagBlocksLowerTriangular" | custom-call | tf_op jit(solution)/shard_map/jit(_solve_triangular)/triangular_solve | solution.py:34
  531.0 1.1 fusion.6
  532.1 1.8 convolution_subtract_fusion.2
  533.9 1.1 fusion.24
  535.0 1.1 fusion.8
  536.0 1.0 convolution_subtract_fusion.3
  537.1 1.1 fusion.25
  538.4 19.0 %convolution_subtract_fusion = f32[2048,2048]{1,0:T(8,128)} fusion(f32[2048,2048]{1,0:T(8,128)} %convolution_subtract_fusion.1, f32[128,2048]{1,0:T(8,128)S(1)} %fusion.25, f32[128,2048]{1,0:T(8,128)S(1)} %fusion.8, f32[128,2048]{1,0:T(8,128)S(1)} %fusion.24, f32[128,2048]{1,0:T(8,128)S(1)} %fusion.6), kind=kOutput, calls=%fused_computation.4 | convolution fusion | flops 12890144768 | bytes 37748736 | tf_op jit(solution)/shard_map/dot_general | solution.py:18
  557.5 2.5 maximum_maximum_fusion
  560.0 2.4 pad_maximum_fusion
  562.4 5.3 copy.8
  (56 shorter events, 5.1 us)
Async XLA Ops:
  7.2 106.6 %all-reduce.8.cloned.1.call-start = ((), (), s32[]{:S(2)}) async-start(), calls=%async_computation | async-start | bytes 4194304 | tf_op jit(solution)/shard_map/psum | solution.py:14
  10.3 184.5 %all-reduce.14.cloned.1.call-start = ((), (), s32[]{:S(2)}) async-start(), calls=%async_computation.3 | async-start | bytes 4718592 | tf_op jit(solution)/shard_map/psum | solution.py:29
  113.8 6.5 %copy-start = (f32[2048,256]{1,0:T(8,128)S(1)}, f32[2048,256]{1,0:T(8,128)}, u32[]{:S(2)}) copy-start(f32[2048,256]{1,0:T(8,128)} %all-reduce.8.cloned.1.call-done) | copy-start | bytes 6291460
  138.0 249.0 %all-reduce.10.cloned.1.call-start = ((), (), s32[]{:S(2)}) async-start(), calls=%async_computation.1 | async-start | bytes 4194304 | tf_op jit(solution)/shard_map/psum | solution.py:14
  258.0 2.9 copy-start.8
  260.9 3.2 copy-start.4
  261.9 2.1 copy-start.2
  264.0 18.9 %copy-start.5 = (f32[128,2048]{1,0:T(8,128)}, f32[128,2048]{1,0:T(8,128)S(1)}, u32[]{:S(2)}) copy-start(f32[128,2048]{1,0:T(8,128)S(1)} %fusion.23) | copy-start | bytes 3145732
  286.0 182.2 %all-reduce.12.cloned.1.call-start = ((), (), s32[]{:S(2)}) async-start(), calls=%async_computation.2 | async-start | bytes 4718592 | tf_op jit(solution)/shard_map/psum | solution.py:29
  387.0 6.5 %copy-start.1 = (f32[2048,256]{1,0:T(8,128)S(1)}, f32[2048,256]{1,0:T(8,128)}, u32[]{:S(2)}) copy-start(f32[2048,256]{1,0:T(8,128)} %all-reduce.10.cloned.1.call-done) | copy-start | bytes 6291460
  532.1 2.9 copy-start.9
  538.4 19.1 %copy-start.3 = (f32[128,2048]{1,0:T(8,128)S(1)}, f32[128,2048]{1,0:T(8,128)}, u32[]{:S(2)}) copy-start(f32[128,2048]{1,0:T(8,128)} %copy-done.2) | copy-start | bytes 3145732
  538.4 19.1 %copy-start.6 = (f32[128,2048]{1,0:T(8,128)S(1)}, f32[128,2048]{1,0:T(8,128)}, u32[]{:S(2)}) copy-start(f32[128,2048]{1,0:T(8,128)} %copy-done.5) | copy-start | bytes 3145732
  557.5 2.5 copy-start.7
Sparse Core Ops, SparseCore 0:
  12.2 101.5 all-reduce.7
  138.2 56.5 all-reduce.13
  286.2 100.8 all-reduce.9
  411.6 56.6 all-reduce.11
where the time goes:
time: 583 us; the launch traced here: 575 us
  waiting for transfers between devices  315 us (54%)
  other arithmetic  124 us (21%)
  matrix products  102 us (17%)
  between operations  17.3 us (3%)
  local copies, waits for them, and re-layouts  15.7 us (3%)
    psum x2, waiting for transfers between devices, spread(): return lax.psum(jnp.where(mine, shard, jnp.zeros_like(shard)), axis)  204 us
    psum x2, waiting for transfers between devices, on_device(): lax.psum((product(panel_cols.T, panel_cols), product(panel_cols.T, curren...  110 us
    dot_general x6, matrix products, product(): return jnp.dot(left, right, precision=lax.Precision.HIGHEST)  86.5 us
    another operation x13, other arithmetic, on_device(): lower_factor = jnp.linalg.cholesky(gram_matrix)  68.6 us
    another operation x5, other arithmetic, on_device(): jax.scipy.linalg.solve_triangular(lower_factor, cross_terms, lower=True)  39.7 us
  transfers between devices with their start and end apart: 4, of which 4 were waited for; matrix products, arithmetic and copies ran while one was open for 0% of the time, Pallas kernels for 0%

commit v1 on v0

v1 whole, which is shorter than its diff:
```python
import functools
import math

import jax
import jax.numpy as jnp
from jax import lax
from jax.experimental import pallas as pl
from jax.experimental.pallas import tpu as pltpu
from jax.sharding import PartitionSpec as P

B = 256
PANELS = 2
LANES = 128
SUB = 8
PIECES = 8
CHUNKS = B // LANES
BLOCKS = PANELS * CHUNKS
WIDTH = PANELS * B
MESH = pl.DeviceIdType.MESH
F32 = jnp.float32
ROWS_ROWS = (((0,), (0,)), ((), ()))
ROWS_COLS = (((1,), (0,)), ((), ()))
COLS_COLS = (((1,), (1,)), ((), ()))


def exact_dot(left, right, dims):
    return lax.dot_general(
        left, right, dims, precision=lax.Precision.HIGHEST, preferred_element_type=F32
    )


def split(x):
    high = x.astype(jnp.bfloat16)
    return high, (x - high.astype(F32)).astype(jnp.bfloat16)


def split_dot(left, right, dims):
    dot = functools.partial(lax.dot_general, dimension_numbers=dims, preferred_element_type=F32)
    return dot(left[0], right[0]) + (dot(left[0], right[1]) + dot(left[1], right[0]))


def gather_kernel(n_row, n_col, a_ref, w_ref, z_ref, g_ref, zacc, gacc, zcore, gcore, zmine, gmine,
                  zx, gx, piece_recv, z_send, y_send, core_send, core_recv, x_send, x_recv,
                  back_send, back_recv):
    ny = 1
    while 4 * ny * ny <= n_col:
        ny *= 2
    nz = n_col // ny
    nx = n_row // 2
    row, col = lax.axis_index("row"), lax.axis_index("col")
    zz, yy = col // ny, lax.rem(col, ny)
    xx, core = row // 2, lax.rem(row, 2)
    mate = xx * 2 + 1 - core
    rows, cols = a_ref.shape
    depth = rows // PIECES
    half = cols // 2
    total = CHUNKS * PIECES

    def across_y(d):
        return zz * ny + lax.rem(yy + d, ny)

    def across_x(d):
        return lax.rem(xx + d, nx) * 2 + core

    barrier = pltpu.get_barrier_semaphore()
    greeted = 0
    for d in sorted({1, nz - 1}):
        pl.semaphore_signal(barrier, inc=1, device_id={"col": lax.rem(zz + d, nz) * ny + yy},
                            device_id_type=MESH)
        greeted += 1
    for d in range(1, ny):
        pl.semaphore_signal(barrier, inc=1, device_id={"col": across_y(d)}, device_id_type=MESH)
        greeted += 1
    for d in range(1, nx):
        pl.semaphore_signal(barrier, inc=1, device_id={"row": across_x(d)}, device_id_type=MESH)
        greeted += 1
    pl.semaphore_signal(barrier, inc=1, device_id={"row": mate}, device_id_type=MESH)
    greeted += 1
    pl.semaphore_wait(barrier, greeted)

    def piece(panel, t):
        return w_ref.at[panel * CHUNKS + t // PIECES, pl.ds(lax.rem(t, PIECES) * depth, depth), :]

    def z_copy(panel, t):
        place = piece(panel, t)
        return pltpu.make_async_remote_copy(
            src_ref=place, dst_ref=place, send_sem=z_send.at[t], recv_sem=piece_recv.at[panel, t],
            device_id={"col": col + ny}, device_id_type=MESH)

    def y_copy(panel, t, d):
        place = piece(panel, t)
        return pltpu.make_async_remote_copy(
            src_ref=place, dst_ref=place, send_sem=y_send.at[d - 1, t],
            recv_sem=piece_recv.at[panel, t],
            device_id={"col": across_y(d)}, device_id_type=MESH)

    def pass_on(panel, t):
        @pl.when(zz < nz - 1)
        def _():
            z_copy(panel, t).start()
        for d in range(1, ny):
            y_copy(panel, t, d).start()

    for panel in range(PANELS):
        @pl.when(col == panel)
        def _():
            for j in range(CHUNKS):
                w_ref[panel * CHUNKS + j] = a_ref[:, j * LANES:(j + 1) * LANES]

            def begin(t, carry):
                pass_on(panel, t)
                return carry
            lax.fori_loop(0, total, begin, 0)

    def relay(t):
        for panel in range(PANELS):
            @pl.when((yy == panel) & (zz > 0))
            def _():
                z_copy(panel, t).wait_recv()
                pass_on(panel, t)

    def arrive(t):
        for panel in range(PANELS):
            @pl.when(yy != panel)
            def _():
                y_copy(panel, t, 1).wait_recv()

    def rows_of(panel):
        return slice(panel * LANES, (panel + 1) * LANES)

    def gram_width(j):
        return (j + 1) * LANES

    def core_copies(j):
        other = 1 - core
        z_part = pl.ds(pl.multiple_of(other * half, half), half)
        g_part = pl.ds(pl.multiple_of(other * B, B), gram_width(j))
        return [
            pltpu.make_async_remote_copy(
                src_ref=gacc.at[j, :, g_part], dst_ref=gcore.at[j, :, pl.ds(0, gram_width(j))],
                send_sem=core_send.at[j, 0], recv_sem=core_recv.at[j, 0],
                device_id={"row": mate}, device_id_type=MESH),
            pltpu.make_async_remote_copy(
                src_ref=zacc.at[j, :, z_part], dst_ref=zcore.at[j],
                send_sem=core_send.at[j, 1], recv_sem=core_recv.at[j, 1],
                device_id={"row": mate}, device_id_type=MESH),
        ]

    def x_copies(j, part):
        found = []
        for d in range(1, nx):
            if part == 0:
                width = pl.ds(0, gram_width(j))
                source, target = gmine.at[j, :, width], gx.at[d - 1, j, :, width]
            else:
                source, target = zmine.at[j], zx.at[d - 1, j]
            found.append(pltpu.make_async_remote_copy(
                src_ref=source, dst_ref=target,
                send_sem=x_send.at[d - 1, j, part], recv_sem=x_recv.at[d - 1, j, part],
                device_id={"row": across_x(d)}, device_id_type=MESH))
        return found

    def back_copies(j, part):
        found = []
        for panel in range(PANELS):
            block = pl.ds(panel * B + j * LANES, LANES)
            if part == 0:
                place = g_ref.at[block, pl.ds(pl.multiple_of(core * B, B), gram_width(j))]
            else:
                place = z_ref.at[block, pl.ds(pl.multiple_of(core * half, half), half)]
            found.append(pltpu.make_async_remote_copy(
                src_ref=place, dst_ref=place,
                send_sem=back_send.at[j, part, panel], recv_sem=back_recv.at[j, part, panel],
                device_id={"row": mate}, device_id_type=MESH))
        return found

    def core_sum(j):
        z_part = pl.ds(pl.multiple_of(core * half, half), half)
        g_part = pl.ds(pl.multiple_of(core * B, B), gram_width(j))
        first, second = core_copies(j)
        first.wait_recv()
        gmine[j, :, 0:gram_width(j)] = gacc[j, :, g_part] + gcore[j, :, 0:gram_width(j)]
        for copy in x_copies(j, 0):
            copy.start()
        second.wait_recv()
        zmine[j] = zacc[j, :, z_part] + zcore[j]
        for copy in x_copies(j, 1):
            copy.start()

    def x_sum(j, part):
        for copy in x_copies(j, part):
            copy.wait_recv()
        if part == 0:
            summed = gmine[j, :, 0:gram_width(j)]
            for d in range(nx - 1):
                summed = summed + gx[d, j, :, 0:gram_width(j)]
            for panel in range(PANELS):
                g_ref[panel * B + j * LANES:panel * B + (j + 1) * LANES,
                      pl.ds(pl.multiple_of(core * B, B), gram_width(j))] = summed[rows_of(panel)]
        else:
            for panel in range(PANELS):
                summed = zmine[j, rows_of(panel)]
                for d in range(nx - 1):
                    summed = summed + zx[d, j, rows_of(panel)]
                z_ref[panel * B + j * LANES:panel * B + (j + 1) * LANES,
                      pl.ds(pl.multiple_of(core * half, half), half)] = summed
        for copy in back_copies(j, part):
            copy.start()

    zacc[...] = jnp.zeros_like(zacc)
    gacc[...] = jnp.zeros_like(gacc)
    g_ref[...] = jnp.zeros_like(g_ref)
    relay(0)
    for j in range(CHUNKS):
        def step(i, carry, j=j):
            t = j * PIECES + i

            @pl.when(t + 1 < total)
            def _():
                relay(t + 1)
            arrive(t)
            here = pl.ds(i * depth, depth)
            fresh = jnp.concatenate(
                [w_ref[panel * CHUNKS + j, here, :] for panel in range(PANELS)], axis=1)
            left = split(fresh)
            for k in range(0, cols, 512):
                right = split(a_ref[here, k:k + 512])
                zacc[j, :, k:k + 512] += split_dot(left, right, ROWS_ROWS)
            for q in range(j + 1):
                old = fresh if q == j else jnp.concatenate(
                    [w_ref[panel * CHUNKS + q, here, :] for panel in range(PANELS)], axis=1)
                gram = exact_dot(fresh, old, ROWS_ROWS)
                for panel in range(PANELS):
                    spot = panel * B + q * LANES
                    gacc[j, :, spot:spot + LANES] += gram[:, rows_of(panel)]
            if j > 0:
                @pl.when(i == 1)
                def _():
                    core_sum(j - 1)
            return carry
        lax.fori_loop(0, PIECES, step, 0)
        for copy in core_copies(j):
            copy.start()
    last = CHUNKS - 1
    core_sum(last)
    for j in range(last):
        x_sum(j, 0)
        x_sum(j, 1)
    x_sum(last, 0)
    x_sum(last, 1)

    def waits(t, carry):
        for panel in range(PANELS):
            @pl.when(yy == panel)
            def _():
                @pl.when(zz < nz - 1)
                def _():
                    z_copy(panel, t).wait_send()
                for d in range(1, ny):
                    y_copy(panel, t, d).wait_send()
        return carry
    lax.fori_loop(0, total, waits, 0)
    for j in range(CHUNKS):
        for copy in core_copies(j):
            copy.wait_send()
        for part in range(2):
            for copy in x_copies(j, part):
                copy.wait_send()
            for copy in back_copies(j, part):
                copy.wait_send()
    for j in range(CHUNKS):
        for part in range(2):
            for panel in range(PANELS):
                block = pl.ds(panel * B + j * LANES, LANES)
                if part == 0:
                    place = g_ref.at[block, pl.ds(pl.multiple_of((1 - core) * B, B), gram_width(j))]
                else:
                    place = z_ref.at[block, pl.ds(pl.multiple_of((1 - core) * half, half), half)]
                pltpu.make_async_remote_copy(
                    src_ref=place, dst_ref=place,
                    send_sem=back_send.at[j, part, panel], recv_sem=back_recv.at[j, part, panel],
                    device_id={"row": mate}, device_id_type=MESH).wait_recv()


def invert_factor(m_ref):
    lane = lax.broadcasted_iota(jnp.int32, (SUB, 2 * LANES), 1)
    sub = lax.broadcasted_iota(jnp.int32, (SUB, 2 * LANES), 0)
    for g in range(LANES // SUB):
        base = g * SUB
        strip = m_ref[base:base + SUB, :]
        for k in range(SUB - 1):
            ratio = strip[:, base + k:base + k + 1] / strip[k:k + 1, base + k:base + k + 1]
            strip = strip - jnp.where(sub > k, ratio, 0.0) * strip[k:k + 1, :]
        pivots = jnp.sum(jnp.where(lane == base + sub, strip, 0.0), axis=1, keepdims=True)
        strip = strip / jnp.sqrt(pivots)
        m_ref[base:base + SUB, :] = strip
        if base + SUB < LANES:
            ahead = jnp.where(lane[:, :LANES] >= base + SUB, strip[:, :LANES], 0.0)
            change = exact_dot(ahead, strip, ROWS_ROWS)
            m_ref[base + SUB:, :] -= change[base + SUB:, :]


def factor(g_ref, s_ref, m_ref):
    def tile(i, j):
        return g_ref[i * LANES:(i + 1) * LANES, j * LANES:(j + 1) * LANES]

    for i in range(BLOCKS):
        for j in range(BLOCKS):
            known = j % CHUNKS <= i % CHUNKS
            s_ref[i * LANES:(i + 1) * LANES, j * LANES:(j + 1) * LANES] = (
                tile(i, j) if known else tile(j, i).T)
    ident = (lax.broadcasted_iota(jnp.int32, (WIDTH, WIDTH), 0)
             == lax.broadcasted_iota(jnp.int32, (WIDTH, WIDTH), 1)).astype(F32)
    s_ref[:, WIDTH:] = ident
    for b in range(BLOCKS):
        here = slice(b * LANES, (b + 1) * LANES)
        m_ref[:, :LANES] = s_ref[here, here]
        m_ref[:, LANES:] = ident[:LANES, :LANES]
        invert_factor(m_ref)
        strip = exact_dot(m_ref[:, LANES:], s_ref[here, :], ROWS_COLS)
        s_ref[here, :] = strip
        if b + 1 < BLOCKS:
            below = slice((b + 1) * LANES, WIDTH)
            s_ref[below, :] -= exact_dot(strip[:, below], strip, ROWS_ROWS)


def update_kernel(scale, g_ref, z_ref, w_ref, a_ref, r_ref, q_ref, t_ref,
                  s_ref, m_ref, inv_high, inv_low, r_high, r_low):
    cols = a_ref.shape[1]

    @pl.when(pl.program_id(0) == 0)
    def _():
        factor(g_ref, s_ref, m_ref)
        inverse = split(s_ref[:, WIDTH:])
        inv_high[...] = inverse[0]
        inv_low[...] = inverse[1]
        for k in range(0, cols, 512):
            r = split_dot(inverse, split(z_ref[:, k:k + 512]), ROWS_COLS)
            r_ref[:, k:k + 512] = r
            high, low = split(r)
            r_high[:, k:k + 512] = high
            r_low[:, k:k + 512] = low

    w = jnp.concatenate([w_ref[i] for i in range(BLOCKS)], axis=1)
    q = split_dot(split(w), (inv_high[...], inv_low[...]), COLS_COLS)
    q_ref[...] = q * scale
    q = split(q)
    for k in range(0, cols, 512):
        r = r_high[:, k:k + 512], r_low[:, k:k + 512]
        t_ref[:, k:k + 512] = a_ref[:, k:k + 512] - split_dot(q, r, ROWS_COLS)


def on_device(n_row, n_col, matrix):
    rows, cols = matrix.shape
    nx = n_row // 2
    half = cols // 2
    vmem = pl.BlockSpec(memory_space=pltpu.VMEM)
    dma = pltpu.SemaphoreType.DMA
    total = CHUNKS * PIECES
    ny = 1
    while 4 * ny * ny <= n_col:
        ny *= 2
    stacked = PANELS * LANES
    w, z, g = pl.pallas_call(
        functools.partial(gather_kernel, n_row, n_col),
        out_shape=(
            jax.ShapeDtypeStruct((BLOCKS, rows, LANES), F32),
            jax.ShapeDtypeStruct((WIDTH, cols), F32),
            jax.ShapeDtypeStruct((WIDTH, WIDTH), F32),
        ),
        in_specs=[vmem],
        out_specs=(vmem, vmem, vmem),
        scratch_shapes=[
            pltpu.VMEM((CHUNKS, stacked, cols), F32),
            pltpu.VMEM((CHUNKS, stacked, WIDTH), F32),
            pltpu.VMEM((CHUNKS, stacked, half), F32),
            pltpu.VMEM((CHUNKS, stacked, B), F32),
            pltpu.VMEM((CHUNKS, stacked, half), F32),
            pltpu.VMEM((CHUNKS, stacked, B), F32),
            pltpu.VMEM((nx - 1, CHUNKS, stacked, half), F32),
            pltpu.VMEM((nx - 1, CHUNKS, stacked, B), F32),
            dma((PANELS, total)),
            dma((total,)),
            dma((ny - 1, total)),
            dma((CHUNKS, 2)),
            dma((CHUNKS, 2)),
            dma((nx - 1, CHUNKS, 2)),
            dma((nx - 1, CHUNKS, 2)),
            dma((CHUNKS, 2, PANELS)),
            dma((CHUNKS, 2, PANELS)),
        ],
        compiler_params=pltpu.CompilerParams(
            collective_id=0, has_side_effects=True, vmem_limit_bytes=60 * 1024 * 1024),
        name="gather_and_multiply",
    )(matrix)
    step = 256
    return pl.pallas_call(
        functools.partial(update_kernel, math.sqrt(rows * n_row)),
        grid=(rows // step,),
        out_shape=(
            jax.ShapeDtypeStruct((WIDTH, cols), F32),
            jax.ShapeDtypeStruct((rows, WIDTH), F32),
            jax.ShapeDtypeStruct((rows, cols), F32),
        ),
        in_specs=[
            vmem,
            vmem,
            pl.BlockSpec((BLOCKS, step, LANES), lambda i: (0, i, 0)),
            pl.BlockSpec((step, cols), lambda i: (i, 0)),
        ],
        out_specs=(
            pl.BlockSpec((WIDTH, cols), lambda i: (0, 0)),
            pl.BlockSpec((step, WIDTH), lambda i: (i, 0)),
            pl.BlockSpec((step, cols), lambda i: (i, 0)),
        ),
        scratch_shapes=[
            pltpu.VMEM((WIDTH, 2 * WIDTH), F32),
            pltpu.VMEM((LANES, 2 * LANES), F32),
            pltpu.VMEM((WIDTH, WIDTH), jnp.bfloat16),
            pltpu.VMEM((WIDTH, WIDTH), jnp.bfloat16),
            pltpu.VMEM((WIDTH, cols), jnp.bfloat16),
            pltpu.VMEM((WIDTH, cols), jnp.bfloat16),
        ],
        compiler_params=pltpu.CompilerParams(vmem_limit_bytes=60 * 1024 * 1024),
        name="factor_and_update",
    )(g, z, w, matrix)


def solution(mesh):
    sizes = mesh.shape
    placed = (P("row", "col"),)
    return jax.shard_map(
        functools.partial(on_device, sizes["row"], sizes["col"]),
        mesh=mesh,
        in_specs=placed,
        out_specs=(P(None, "col"), P("row", None), P("row", "col")),
        check_vma=False,
    )
```

time: 583 us -> 212 us (0.36); the launches traced: 575 us -> 211 us
  waiting for transfers between devices: 315 us -> 0 us
  Pallas kernels: 0 us -> 210 us
  other arithmetic: 124 us -> 0 us
  matrix products: 102 us -> 0 us
  between operations: 17.3 us -> 0.64 us
  local copies, waits for them, and re-layouts: 15.7 us -> 0 us
    psum x4 -> x0, waiting for transfers between devices: 315 us -> none  [the longest x2 204 us: spread(): return lax.psum(jnp.where(mine, shard, jnp.zeros_like(shard)), axis)]
    pallas_call x0 -> x2, Pallas kernels: none -> 210 us  [the longest x1 116 us: on_device(): pl.pallas_call(functools.partial(gather_kernel, n_row, n_col), out_shape=...]
    another operation x18 -> x0, other arithmetic: 108 us -> none  [the longest x13 68.6 us: on_device(): lower_factor = jnp.linalg.cholesky(gram_matrix)]
    dot_general x6 -> x0, matrix products: 86.5 us -> none  [product(): return jnp.dot(left, right, precision=lax.Precision.HIGHEST)]
    another operation x16 -> x0, matrix products: 15.1 us -> none  [the longest x6 7.91 us: on_device(): jax.scipy.linalg.solve_triangular(lower_factor, panel_cols.T, lower=True)]
    another operation x19 -> x0, local copies, waits for them, and re-layouts: 8.15 us -> none  [the longest x15 8.1 us: on_device(): jax.scipy.linalg.solve_triangular(lower_factor, cross_terms, lower=True)]
    select_n x2 -> x0, other arithmetic: 6.09 us -> none  [spread(): return lax.psum(jnp.where(mine, shard, jnp.zeros_like(shard)), axis)]
  transfers between devices with their start and end apart: 4 -> 0, of which waited for: 4 -> 0; matrix products, arithmetic and copies ran while one was open for 0% -> 0% of each run, Pallas kernels for 0% -> 0%
where the time goes in v1:
time: 212 us; the launch traced here: 211 us
  Pallas kernels  210 us (99%)
    pallas_call x1, Pallas kernels, on_device(): pl.pallas_call(functools.partial(gather_kernel, n_row, n_col), out_shape=...  116 us
    pallas_call x1, Pallas kernels, on_device(): pl.pallas_call(functools.partial(update_kernel, math.sqrt(rows * n_row)),...  94.6 us

profile of v1, /device:TPU:29, one launch (start us, length us, event | category | flops | bytes accessed | tf_op | source)
XLA Modules:
  0.0 211.0 jit_solution(16165196541002728938)
XLA Ops:
  0.6 115.8 %gather_and_multiply.1 = (f32[4,2048,128]{2,1,0:T(8,128)}, f32[512,2048]{1,0:T(8,128)}, f32[512,512]{1,0:T(8,128)}) custom-call(f32[2048,2048]{1,0:T(8,128)} %a_ref.3), custom_call_target="tpu_custom_call" | custom-call | tf_op jit(solution)/shard_map/gather_and_multiply/pallas_call | solution.py:364
  116.5 94.6 %factor_and_update.1 = (f32[512,2048]{1,0:T(8,128)}, f32[2048,512]{1,0:T(8,128)}, f32[2048,2048]{1,0:T(8,128)}) custom-call(f32[512,512]{1,0:T(8,128)} %get-tuple-element.6.g_ref, f32[512,2048]{1,0:T(8,128)} %get-tuple-element.7.z_ref, f32[4,2048,128]{2,1,0:T(8,128)} %get-tuple-element.8.w_ref, f32[2048,2048]{1,0:T(8,128)} %a_ref.3), custom_call_target="tpu_custom_call" | custom-call | tf_op jit(solution)/shard_map/factor_and_update/pallas_call | solution.py:397

commit v2 on v1

--- a/solution.py
+++ b/solution.py
@@ -12,7 +12,8 @@
 PANELS = 2
 LANES = 128
 SUB = 8
-PIECES = 8
+PIECES = 16
+GROUP = 2
 CHUNKS = B // LANES
 BLOCKS = PANELS * CHUNKS
 WIDTH = PANELS * B
@@ -39,7 +40,7 @@
     return dot(left[0], right[0]) + (dot(left[0], right[1]) + dot(left[1], right[0]))
 
 
-def gather_kernel(n_row, n_col, a_ref, w_ref, z_ref, g_ref, zacc, gacc, zcore, gcore, zmine, gmine,
+def gather_kernel(n_row, n_col, a_ref, w_ref, z_ref, inv_ref, g_ref, s_ref, m_ref, zacc, gacc, zcore, gcore, zmine, gmine,
                   zx, gx, piece_recv, z_send, y_send, core_send, core_recv, x_send, x_recv,
                   back_send, back_recv):
     ny = 1
@@ -173,6 +174,18 @@
                 send_sem=back_send.at[j, part, panel], recv_sem=back_recv.at[j, part, panel],
                 device_id={"row": mate}, device_id_type=MESH))
         return found
+
+    def back_arrive(j, part):
+        for panel in range(PANELS):
+            block = pl.ds(panel * B + j * LANES, LANES)
+            if part == 0:
+                place = g_ref.at[block, pl.ds(pl.multiple_of((1 - core) * B, B), gram_width(j))]
+            else:
+                place = z_ref.at[block, pl.ds(pl.multiple_of((1 - core) * half, half), half)]
+            pltpu.make_async_remote_copy(
+                src_ref=place, dst_ref=place,
+                send_sem=back_send.at[j, part, panel], recv_sem=back_recv.at[j, part, panel],
+                device_id={"row": mate}, device_id_type=MESH).wait_recv()
 
     def core_sum(j):
         z_part = pl.ds(pl.multiple_of(core * half, half), half)
@@ -210,22 +223,25 @@
     zacc[...] = jnp.zeros_like(zacc)
     gacc[...] = jnp.zeros_like(gacc)
     g_ref[...] = jnp.zeros_like(g_ref)
-    relay(0)
+    for t in range(GROUP):
+        relay(t)
     for j in range(CHUNKS):
         def step(i, carry, j=j):
-            t = j * PIECES + i
-
-            @pl.when(t + 1 < total)
-            def _():
-                relay(t + 1)
-            arrive(t)
-            here = pl.ds(i * depth, depth)
+            t = j * PIECES + GROUP * i
+            here = pl.ds(i * GROUP * depth, GROUP * depth)
+            for u in range(GROUP):
+                arrive(t + u)
             fresh = jnp.concatenate(
                 [w_ref[panel * CHUNKS + j, here, :] for panel in range(PANELS)], axis=1)
             left = split(fresh)
-            for k in range(0, cols, 512):
-                right = split(a_ref[here, k:k + 512])
-                zacc[j, :, k:k + 512] += split_dot(left, right, ROWS_ROWS)
+            span = cols // GROUP
+            for u in range(GROUP):
+                @pl.when(t + GROUP + u < total)
+                def _():
+                    relay(t + GROUP + u)
+                for k in range(u * span, (u + 1) * span, 512):
+                    right = split(a_ref[here, k:k + 512])
+                    zacc[j, :, k:k + 512] += split_dot(left, right, ROWS_ROWS)
             for q in range(j + 1):
                 old = fresh if q == j else jnp.concatenate(
                     [w_ref[panel * CHUNKS + q, here, :] for panel in range(PANELS)], axis=1)
@@ -238,15 +254,19 @@
                 def _():
                     core_sum(j - 1)
             return carry
-        lax.fori_loop(0, PIECES, step, 0)
+        lax.fori_loop(0, PIECES // GROUP, step, 0)
         for copy in core_copies(j):
             copy.start()
     last = CHUNKS - 1
     core_sum(last)
+    for j in range(CHUNKS):
+        x_sum(j, 0)
+    for j in range(CHUNKS):
+        back_arrive(j, 0)
     for j in range(last):
-        x_sum(j, 0)
         x_sum(j, 1)
-    x_sum(last, 0)
+    factor(g_ref, s_ref, m_ref)
+    inv_ref[...] = s_ref[:, WIDTH:]
     x_sum(last, 1)
 
     def waits(t, carry):
@@ -269,35 +289,63 @@
             for copy in back_copies(j, part):
                 copy.wait_send()
     for j in range(CHUNKS):
-        for part in range(2):
-            for panel in range(PANELS):
-                block = pl.ds(panel * B + j * LANES, LANES)
-                if part == 0:
-                    place = g_ref.at[block, pl.ds(pl.multiple_of((1 - core) * B, B), gram_width(j))]
-                else:
-                    place = z_ref.at[block, pl.ds(pl.multiple_of((1 - core) * half, half), half)]
-                pltpu.make_async_remote_copy(
-                    src_ref=place, dst_ref=place,
-                    send_sem=back_send.at[j, part, panel], recv_sem=back_recv.at[j, part, panel],
-                    device_id={"row": mate}, device_id_type=MESH).wait_recv()
+        back_arrive(j, 1)
 
 
 def invert_factor(m_ref):
-    lane = lax.broadcasted_iota(jnp.int32, (SUB, 2 * LANES), 1)
-    sub = lax.broadcasted_iota(jnp.int32, (SUB, 2 * LANES), 0)
+    lane = lax.broadcasted_iota(jnp.int32, (SUB, LANES), 1)
+    sub = lax.broadcasted_iota(jnp.int32, (SUB, LANES), 0)
+    strip = m_ref[0:SUB, :]
     for g in range(LANES // SUB):
         base = g * SUB
-        strip = m_ref[base:base + SUB, :]
-        for k in range(SUB - 1):
-            ratio = strip[:, base + k:base + k + 1] / strip[k:k + 1, base + k:base + k + 1]
-            strip = strip - jnp.where(sub > k, ratio, 0.0) * strip[k:k + 1, :]
-        pivots = jnp.sum(jnp.where(lane == base + sub, strip, 0.0), axis=1, keepdims=True)
-        strip = strip / jnp.sqrt(pivots)
-        m_ref[base:base + SUB, :] = strip
-        if base + SUB < LANES:
-            ahead = jnp.where(lane[:, :LANES] >= base + SUB, strip[:, :LANES], 0.0)
-            change = exact_dot(ahead, strip, ROWS_ROWS)
-            m_ref[base + SUB:, :] -= change[base + SUB:, :]
+        left, right = strip[:, :LANES], strip[:, LANES:]
+        entry = {}
+        for k in range(SUB):
+            column = jnp.broadcast_to(left[:, base + k:base + k + 1], (SUB, LANES))
+            for i in range(k, SUB):
+                entry[i, k] = jnp.broadcast_to(column[i:i + 1, :], (SUB, LANES))
+        low, inv = {}, {}
+        for k in range(SUB):
+            pivot = entry[k, k]
+            guess = lax.rsqrt(pivot)
+            guess = guess * (1.5 - (0.5 * pivot) * guess * guess)
+            inv[k, k] = guess
+            for i in range(k + 1, SUB):
+                low[i, k] = entry[i, k] * guess
+            for j in range(k + 1, SUB):
+                for i in range(j, SUB):
+                    entry[i, j] = entry[i, j] - low[i, k] * low[j, k]
+        for i in range(SUB):
+            for j in range(i):
+                acc = low[i, j] * inv[j, j]
+                for k in range(j + 1, i):
+                    acc = acc + low[i, k] * inv[k, j]
+                inv[i, j] = -acc * inv[i, i]
+        done = []
+        for side in (left, right):
+            acc = None
+            for j in range(SUB):
+                weight = jnp.zeros((SUB, LANES), F32)
+                for i in range(j, SUB):
+                    weight = jnp.where(sub == i, inv[i, j], weight)
+                term = weight * side[j:j + 1, :]
+                acc = term if acc is None else acc + term
+            done.append(acc)
+        m_ref[base:base + SUB, :LANES] = done[0]
+        m_ref[base:base + SUB, LANES:] = done[1]
+        after = base + SUB
+        if after < LANES:
+            fresh = [m_ref[after:after + SUB, :LANES], m_ref[after:after + SUB, LANES:]]
+            for i in range(SUB):
+                column = jnp.broadcast_to(done[0][:, after + i:after + i + 1], (SUB, LANES))
+                for side in range(2):
+                    change = jnp.sum(column * done[side], axis=0, keepdims=True)
+                    fresh[side] = jnp.where(sub == i, fresh[side] - change, fresh[side])
+            strip = jnp.concatenate(fresh, axis=1)
+        if after + SUB < LANES:
+            ahead = jnp.where(lane >= after + SUB, done[0], 0.0)
+            change = exact_dot(ahead, jnp.concatenate(done, axis=1), ROWS_ROWS)
+            m_ref[after + SUB:, :] -= change[after + SUB:, :]
 
 
 def factor(g_ref, s_ref, m_ref):
@@ -312,26 +360,31 @@
     ident = (lax.broadcasted_iota(jnp.int32, (WIDTH, WIDTH), 0)
              == lax.broadcasted_iota(jnp.int32, (WIDTH, WIDTH), 1)).astype(F32)
     s_ref[:, WIDTH:] = ident
-    for b in range(BLOCKS):
-        here = slice(b * LANES, (b + 1) * LANES)
+    block_of = lax.broadcasted_iota(jnp.int32, (LANES, WIDTH), 1) // LANES
+
+    def eliminate(b, carry):
+        here = pl.ds(pl.multiple_of(b * LANES, LANES), LANES)
         m_ref[:, :LANES] = s_ref[here, here]
         m_ref[:, LANES:] = ident[:LANES, :LANES]
         invert_factor(m_ref)
         strip = exact_dot(m_ref[:, LANES:], s_ref[here, :], ROWS_COLS)
         s_ref[here, :] = strip
-        if b + 1 < BLOCKS:
-            below = slice((b + 1) * LANES, WIDTH)
-            s_ref[below, :] -= exact_dot(strip[:, below], strip, ROWS_ROWS)
-
-
-def update_kernel(scale, g_ref, z_ref, w_ref, a_ref, r_ref, q_ref, t_ref,
-                  s_ref, m_ref, inv_high, inv_low, r_high, r_low):
+
+        @pl.when(b + 1 < BLOCKS)
+        def _():
+            ahead = jnp.where(block_of > b, strip[:, :WIDTH], 0.0)
+            s_ref[...] -= exact_dot(ahead, strip, ROWS_ROWS)
+        return carry
+    lax.fori_loop(0, BLOCKS, eliminate, 0)
+
+
+def update_kernel(scale, inv_ref, z_ref, w_ref, a_ref, r_ref, q_ref, t_ref,
+                  inv_high, inv_low, r_high, r_low):
     cols = a_ref.shape[1]
 
     @pl.when(pl.program_id(0) == 0)
     def _():
-        factor(g_ref, s_ref, m_ref)
-        inverse = split(s_ref[:, WIDTH:])
+        inverse = split(inv_ref[...])
         inv_high[...] = inverse[0]
         inv_low[...] = inverse[1]
         for k in range(0, cols, 512):
@@ -361,7 +414,7 @@
     while 4 * ny * ny <= n_col:
         ny *= 2
     stacked = PANELS * LANES
-    w, z, g = pl.pallas_call(
+    w, z, inverse = pl.pallas_call(
         functools.partial(gather_kernel, n_row, n_col),
         out_shape=(
             jax.ShapeDtypeStruct((BLOCKS, rows, LANES), F32),
@@ -371,6 +424,9 @@
         in_specs=[vmem],
         out_specs=(vmem, vmem, vmem),
         scratch_shapes=[
+            pltpu.VMEM((WIDTH, WIDTH), F32),
+            pltpu.VMEM((WIDTH, 2 * WIDTH), F32),
+            pltpu.VMEM((LANES, 2 * LANES), F32),
             pltpu.VMEM((CHUNKS, stacked, cols), F32),
             pltpu.VMEM((CHUNKS, stacked, WIDTH), F32),
             pltpu.VMEM((CHUNKS, stacked, half), F32),
@@ -414,8 +470,6 @@
             pl.BlockSpec((step, cols), lambda i: (i, 0)),
         ),
         scratch_shapes=[
-            pltpu.VMEM((WIDTH, 2 * WIDTH), F32),
-            pltpu.VMEM((LANES, 2 * LANES), F32),
             pltpu.VMEM((WIDTH, WIDTH), jnp.bfloat16),
             pltpu.VMEM((WIDTH, WIDTH), jnp.bfloat16),
             pltpu.VMEM((WIDTH, cols), jnp.bfloat16),
@@ -423,7 +477,7 @@
         ],
         compiler_params=pltpu.CompilerParams(vmem_limit_bytes=60 * 1024 * 1024),
         name="factor_and_update",
-    )(g, z, w, matrix)
+    )(inverse, z, w, matrix)
 
 
 def solution(mesh):

time: 212 us -> 176 us (0.83)
  Pallas kernels: 210 us -> 175 us
    pallas_call x1, Pallas kernels: 94.6 us -> 28.4 us  [on_device(): pl.pallas_call(functools.partial(update_kernel, math.sqrt(rows * n_row)),...]
    pallas_call x1, Pallas kernels: 116 us -> 147 us  [on_device(): pl.pallas_call(functools.partial(gather_kernel, n_row, n_col), out_shape=...]
where the time goes in v2:
time: 176 us
  Pallas kernels  175 us (99%)
    pallas_call x1, Pallas kernels, on_device(): pl.pallas_call(functools.partial(gather_kernel, n_row, n_col), out_shape=...  147 us
    pallas_call x1, Pallas kernels, on_device(): pl.pallas_call(functools.partial(update_kernel, math.sqrt(rows * n_row)),...  28.4 us

profile of v2, /device:TPU:29, one launch (start us, length us, event | category | flops | bytes accessed | tf_op | source)
XLA Modules:
  0.0 176.0 jit_solution(13867444689304761679)
XLA Ops:
  0.6 147.0 %gather_and_multiply.1 = (f32[4,2048,128]{2,1,0:T(8,128)}, f32[512,2048]{1,0:T(8,128)}, f32[512,512]{1,0:T(8,128)}) custom-call(f32[2048,2048]{1,0:T(8,128)} %a_ref.3), custom_call_target="tpu_custom_call" | custom-call | tf_op jit(solution)/shard_map/gather_and_multiply/pallas_call | solution.py:417
  147.6 28.4 %factor_and_update.1 = (f32[512,2048]{1,0:T(8,128)}, f32[2048,512]{1,0:T(8,128)}, f32[2048,2048]{1,0:T(8,128)}) custom-call(f32[512,512]{1,0:T(8,128)} %get-tuple-element.6.inv_ref, f32[512,2048]{1,0:T(8,128)} %get-tuple-element.7.z_ref, f32[4,2048,128]{2,1,0:T(8,128)} %get-tuple-element.8.w_ref, f32[2048,2048]{1,0:T(8,128)} %a_ref.3), custom_call_target="tpu_custom_call" | custom-call | tf_op jit(solution)/shard_map/factor_and_update/pallas_call | solution.py:453

commit v3 on v2

--- a/solution.py
+++ b/solution.py
@@ -14,6 +14,7 @@
 SUB = 8
 PIECES = 16
 GROUP = 2
+AHEAD = 3
 CHUNKS = B // LANES
 BLOCKS = PANELS * CHUNKS
 WIDTH = PANELS * B
@@ -40,7 +41,7 @@
     return dot(left[0], right[0]) + (dot(left[0], right[1]) + dot(left[1], right[0]))
 
 
-def gather_kernel(n_row, n_col, a_ref, w_ref, z_ref, inv_ref, g_ref, s_ref, m_ref, zacc, gacc, zcore, gcore, zmine, gmine,
+def gather_kernel(n_row, n_col, a_hbm, w_ref, z_ref, inv_ref, a_ref, a_sem, p_sem, g_ref, s_ref, m_ref, zacc, gacc, zcore, gcore, zmine, gmine,
                   zx, gx, piece_recv, z_send, y_send, core_send, core_recv, x_send, x_recv,
                   back_send, back_recv):
     ny = 1
@@ -52,7 +53,7 @@
     zz, yy = col // ny, lax.rem(col, ny)
     xx, core = row // 2, lax.rem(row, 2)
     mate = xx * 2 + 1 - core
-    rows, cols = a_ref.shape
+    rows, cols = a_hbm.shape
     depth = rows // PIECES
     half = cols // 2
     total = CHUNKS * PIECES
@@ -62,6 +63,19 @@
 
     def across_x(d):
         return lax.rem(xx + d, nx) * 2 + core
+
+    def panel_copies(panel):
+        return [pltpu.make_async_copy(a_hbm.at[:, pl.ds(j * LANES, LANES)],
+                                      w_ref.at[panel * CHUNKS + j], p_sem.at[j])
+                for j in range(CHUNKS)]
+
+    for panel in range(PANELS):
+        @pl.when(col == panel)
+        def _():
+            for copy in panel_copies(panel):
+                copy.start()
+    load = pltpu.make_async_copy(a_hbm, a_ref, a_sem)
+    load.start()
 
     barrier = pltpu.get_barrier_semaphore()
     greeted = 0
@@ -105,13 +119,12 @@
     for panel in range(PANELS):
         @pl.when(col == panel)
         def _():
-            for j in range(CHUNKS):
-                w_ref[panel * CHUNKS + j] = a_ref[:, j * LANES:(j + 1) * LANES]
-
             def begin(t, carry):
                 pass_on(panel, t)
                 return carry
-            lax.fori_loop(0, total, begin, 0)
+            for j, copy in enumerate(panel_copies(panel)):
+                copy.wait()
+                lax.fori_loop(j * PIECES, (j + 1) * PIECES, begin, 0)
 
     def relay(t):
         for panel in range(PANELS):
@@ -223,29 +236,36 @@
     zacc[...] = jnp.zeros_like(zacc)
     gacc[...] = jnp.zeros_like(gacc)
     g_ref[...] = jnp.zeros_like(g_ref)
-    for t in range(GROUP):
+    for t in range(AHEAD):
         relay(t)
+    load.wait()
     for j in range(CHUNKS):
         def step(i, carry, j=j):
             t = j * PIECES + GROUP * i
             here = pl.ds(i * GROUP * depth, GROUP * depth)
+
+            @pl.when(t + AHEAD < total)
+            def _():
+                relay(t + AHEAD)
             for u in range(GROUP):
                 arrive(t + u)
             fresh = jnp.concatenate(
                 [w_ref[panel * CHUNKS + j, here, :] for panel in range(PANELS)], axis=1)
-            left = split(fresh)
+            turned = fresh.T
+            left = split(turned)
             span = cols // GROUP
             for u in range(GROUP):
-                @pl.when(t + GROUP + u < total)
-                def _():
-                    relay(t + GROUP + u)
+                if u > 0:
+                    @pl.when(t + AHEAD + u < total)
+                    def _():
+                        relay(t + AHEAD + u)
                 for k in range(u * span, (u + 1) * span, 512):
                     right = split(a_ref[here, k:k + 512])
-                    zacc[j, :, k:k + 512] += split_dot(left, right, ROWS_ROWS)
+                    zacc[j, :, k:k + 512] += split_dot(left, right, ROWS_COLS)
             for q in range(j + 1):
                 old = fresh if q == j else jnp.concatenate(
                     [w_ref[panel * CHUNKS + q, here, :] for panel in range(PANELS)], axis=1)
-                gram = exact_dot(fresh, old, ROWS_ROWS)
+                gram = exact_dot(turned, old, ROWS_COLS)
                 for panel in range(PANELS):
                     spot = panel * B + q * LANES
                     gacc[j, :, spot:spot + LANES] += gram[:, rows_of(panel)]
@@ -421,9 +441,12 @@
             jax.ShapeDtypeStruct((WIDTH, cols), F32),
             jax.ShapeDtypeStruct((WIDTH, WIDTH), F32),
         ),
-        in_specs=[vmem],
+        in_specs=[pl.BlockSpec(memory_space=pl.ANY)],
         out_specs=(vmem, vmem, vmem),
         scratch_shapes=[
+            pltpu.VMEM((rows, cols), F32),
+            dma,
+            dma((CHUNKS,)),
             pltpu.VMEM((WIDTH, WIDTH), F32),
             pltpu.VMEM((WIDTH, 2 * WIDTH), F32),
             pltpu.VMEM((LANES, 2 * LANES), F32),

time: 176 us -> 150 us (0.85)
  Pallas kernels: 175 us -> 149 us
    pallas_call x1, Pallas kernels: 147 us -> 121 us  [on_device(): pl.pallas_call(functools.partial(gather_kernel, n_row, n_col), out_shape=...]
where the time goes in v3:
time: 150 us
  Pallas kernels  149 us (99%)
    pallas_call x1, Pallas kernels, on_device(): pl.pallas_call(functools.partial(gather_kernel, n_row, n_col), out_shape=...  121 us
    pallas_call x1, Pallas kernels, on_device(): pl.pallas_call(functools.partial(update_kernel, math.sqrt(rows * n_row)),...  28.4 us

profile of v3, /device:TPU:29, one launch (start us, length us, event | category | flops | bytes accessed | tf_op | source)
XLA Modules:
  0.0 149.7 jit_solution(5639597441616861907)
XLA Ops:
  0.6 120.7 %gather_and_multiply.1 = (f32[4,2048,128]{2,1,0:T(8,128)}, f32[512,2048]{1,0:T(8,128)}, f32[512,512]{1,0:T(8,128)}) custom-call(f32[2048,2048]{1,0:T(8,128)} %a_ref.1), custom_call_target="tpu_custom_call" | custom-call | tf_op jit(solution)/shard_map/gather_and_multiply/pallas_call | solution.py:437
  121.3 28.4 %factor_and_update.1 = (f32[512,2048]{1,0:T(8,128)}, f32[2048,512]{1,0:T(8,128)}, f32[2048,2048]{1,0:T(8,128)}) custom-call(f32[512,512]{1,0:T(8,128)} %get-tuple-element.6.inv_ref, f32[512,2048]{1,0:T(8,128)} %get-tuple-element.7.z_ref, f32[4,2048,128]{2,1,0:T(8,128)} %get-tuple-element.8.w_ref, f32[2048,2048]{1,0:T(8,128)} %a_ref.1), custom_call_target="tpu_custom_call" | custom-call | tf_op jit(solution)/shard_map/factor_and_update/pallas_call | solution.py:476

commit v4 on v3

--- a/solution.py
+++ b/solution.py
@@ -15,6 +15,7 @@
 PIECES = 16
 GROUP = 2
 AHEAD = 3
+PARTS = 4
 CHUNKS = B // LANES
 BLOCKS = PANELS * CHUNKS
 WIDTH = PANELS * B
@@ -41,7 +42,8 @@
     return dot(left[0], right[0]) + (dot(left[0], right[1]) + dot(left[1], right[0]))
 
 
-def gather_kernel(n_row, n_col, a_hbm, w_ref, z_ref, inv_ref, a_ref, a_sem, p_sem, g_ref, s_ref, m_ref, zacc, gacc, zcore, gcore, zmine, gmine,
+def gather_kernel(n_row, n_col, a_hbm, w_ref, z_ref, inv_ref, a_ref, a_sem, p_sem, first_ref, own_gram, mate_gram,
+                  pair_gram, x_gram, own_send, own_recv, first_z, first_y, first_recv, g_ref, s_ref, m_ref, zacc, gacc, zcore, gcore, zmine, gmine,
                   zx, gx, piece_recv, z_send, y_send, core_send, core_recv, x_send, x_recv,
                   back_send, back_recv):
     ny = 1
@@ -232,6 +234,68 @@
                       pl.ds(pl.multiple_of(core * half, half), half)] = summed
         for copy in back_copies(j, part):
             copy.start()
+
+    def own_copies():
+        found = [pltpu.make_async_remote_copy(
+            src_ref=own_gram, dst_ref=mate_gram, send_sem=own_send.at[0], recv_sem=own_recv.at[0],
+            device_id={"row": mate}, device_id_type=MESH)]
+        for d in range(1, nx):
+            found.append(pltpu.make_async_remote_copy(
+                src_ref=pair_gram, dst_ref=x_gram.at[d - 1],
+                send_sem=own_send.at[d], recv_sem=own_recv.at[d],
+                device_id={"row": across_x(d)}, device_id_type=MESH))
+        return found
+
+    def first_z_copy(k):
+        place = first_ref.at[pl.ds(k * (B // PARTS), B // PARTS), :]
+        return pltpu.make_async_remote_copy(
+            src_ref=place, dst_ref=place, send_sem=first_z.at[k], recv_sem=first_recv.at[k],
+            device_id={"col": col + ny}, device_id_type=MESH)
+
+    def first_y_copy(k, d):
+        place = first_ref.at[pl.ds(k * (B // PARTS), B // PARTS), :]
+        return pltpu.make_async_remote_copy(
+            src_ref=place, dst_ref=place, send_sem=first_y.at[d - 1, k],
+            recv_sem=first_recv.at[k],
+            device_id={"col": across_y(d)}, device_id_type=MESH)
+
+    def first_on(k):
+        @pl.when(zz < nz - 1)
+        def _():
+            first_z_copy(k).start()
+        for d in range(1, ny):
+            first_y_copy(k, d).start()
+
+    @pl.when(col == 0)
+    def _():
+        own_gram[...] = jnp.zeros_like(own_gram)
+
+        def add(i, carry):
+            here = pl.ds(i * B, B)
+            part = jnp.concatenate([w_ref[j, here, :] for j in range(CHUNKS)], axis=1)
+            own_gram[...] += exact_dot(part.T, part, ROWS_COLS)
+            return carry
+        lax.fori_loop(0, rows // B, add, 0)
+        copies = own_copies()
+        copies[0].start()
+        copies[0].wait_recv()
+        pair_gram[...] = own_gram[...] + mate_gram[...]
+        for copy in copies[1:]:
+            copy.start()
+        for copy in copies[1:]:
+            copy.wait_recv()
+        summed = pair_gram[...]
+        for d in range(nx - 1):
+            summed = summed + x_gram[d]
+        s_ref[:, :WIDTH] = identity()
+        s_ref[:, WIDTH:] = identity()
+        s_ref[0:B, 0:B] = summed
+        eliminate(s_ref, m_ref, 0, CHUNKS)
+        first_ref[...] = s_ref[0:B, WIDTH:WIDTH + B]
+        for k in range(PARTS):
+            first_on(k)
+        for copy in copies:
+            copy.wait_send()
 
     zacc[...] = jnp.zeros_like(zacc)
     gacc[...] = jnp.zeros_like(gacc)
@@ -279,13 +343,22 @@
             copy.start()
     last = CHUNKS - 1
     core_sum(last)
+    for k in range(PARTS):
+        @pl.when((yy == 0) & (zz > 0))
+        def _(k=k):
+            first_z_copy(k).wait_recv()
+            first_on(k)
+
+        @pl.when(yy != 0)
+        def _(k=k):
+            first_y_copy(k, 1).wait_recv()
     for j in range(CHUNKS):
         x_sum(j, 0)
     for j in range(CHUNKS):
         back_arrive(j, 0)
     for j in range(last):
         x_sum(j, 1)
-    factor(g_ref, s_ref, m_ref)
+    factor(g_ref, first_ref, s_ref, m_ref)
     inv_ref[...] = s_ref[:, WIDTH:]
     x_sum(last, 1)
 
@@ -300,6 +373,15 @@
                     y_copy(panel, t, d).wait_send()
         return carry
     lax.fori_loop(0, total, waits, 0)
+
+    @pl.when(yy == 0)
+    def _():
+        for k in range(PARTS):
+            @pl.when(zz < nz - 1)
+            def _(k=k):
+                first_z_copy(k).wait_send()
+            for d in range(1, ny):
+                first_y_copy(k, d).wait_send()
     for j in range(CHUNKS):
         for copy in core_copies(j):
             copy.wait_send()
@@ -368,7 +450,31 @@
             m_ref[after + SUB:, :] -= change[after + SUB:, :]
 
 
-def factor(g_ref, s_ref, m_ref):
+def identity():
+    return (lax.broadcasted_iota(jnp.int32, (WIDTH, WIDTH), 0)
+            == lax.broadcasted_iota(jnp.int32, (WIDTH, WIDTH), 1)).astype(F32)
+
+
+def eliminate(s_ref, m_ref, start, stop):
+    block_of = lax.broadcasted_iota(jnp.int32, (LANES, WIDTH), 1) // LANES
+
+    def one(b, carry):
+        here = pl.ds(pl.multiple_of(b * LANES, LANES), LANES)
+        m_ref[:, :LANES] = s_ref[here, here]
+        m_ref[:, LANES:] = identity()[:LANES, :LANES]
+        invert_factor(m_ref)
+        strip = exact_dot(m_ref[:, LANES:], s_ref[here, :], ROWS_COLS)
+        s_ref[here, :] = strip
+
+        @pl.when(b + 1 < stop)
+        def _():
+            ahead = jnp.where(block_of > b, strip[:, :WIDTH], 0.0)
+            s_ref[...] -= exact_dot(ahead, strip, ROWS_ROWS)
+        return carry
+    lax.fori_loop(start, stop, one, 0)
+
+
+def factor(g_ref, first_ref, s_ref, m_ref):
     def tile(i, j):
         return g_ref[i * LANES:(i + 1) * LANES, j * LANES:(j + 1) * LANES]
 
@@ -377,25 +483,11 @@
             known = j % CHUNKS <= i % CHUNKS
             s_ref[i * LANES:(i + 1) * LANES, j * LANES:(j + 1) * LANES] = (
                 tile(i, j) if known else tile(j, i).T)
-    ident = (lax.broadcasted_iota(jnp.int32, (WIDTH, WIDTH), 0)
-             == lax.broadcasted_iota(jnp.int32, (WIDTH, WIDTH), 1)).astype(F32)
-    s_ref[:, WIDTH:] = ident
-    block_of = lax.broadcasted_iota(jnp.int32, (LANES, WIDTH), 1) // LANES
-
-    def eliminate(b, carry):
-        here = pl.ds(pl.multiple_of(b * LANES, LANES), LANES)
-        m_ref[:, :LANES] = s_ref[here, here]
-        m_ref[:, LANES:] = ident[:LANES, :LANES]
-        invert_factor(m_ref)
-        strip = exact_dot(m_ref[:, LANES:], s_ref[here, :], ROWS_COLS)
-        s_ref[here, :] = strip
-
-        @pl.when(b + 1 < BLOCKS)
-        def _():
-            ahead = jnp.where(block_of > b, strip[:, :WIDTH], 0.0)
-            s_ref[...] -= exact_dot(ahead, strip, ROWS_ROWS)
-        return carry
-    lax.fori_loop(0, BLOCKS, eliminate, 0)
+    s_ref[:, WIDTH:] = identity()
+    strip = exact_dot(first_ref[...], s_ref[0:B, :], ROWS_COLS)
+    s_ref[0:B, :] = strip
+    s_ref[B:WIDTH, :] -= exact_dot(strip[:, B:WIDTH], strip, ROWS_ROWS)
+    eliminate(s_ref, m_ref, CHUNKS, BLOCKS)
 
 
 def update_kernel(scale, inv_ref, z_ref, w_ref, a_ref, r_ref, q_ref, t_ref,
@@ -447,6 +539,16 @@
             pltpu.VMEM((rows, cols), F32),
             dma,
             dma((CHUNKS,)),
+            pltpu.VMEM((B, B), F32),
+            pltpu.VMEM((B, B), F32),
+            pltpu.VMEM((B, B), F32),
+            pltpu.VMEM((B, B), F32),
+            pltpu.VMEM((nx - 1, B, B), F32),
+            dma((nx,)),
+            dma((nx,)),
+            dma((PARTS,)),
+            dma((ny - 1, PARTS)),
+            dma((PARTS,)),
             pltpu.VMEM((WIDTH, WIDTH), F32),
             pltpu.VMEM((WIDTH, 2 * WIDTH), F32),
             pltpu.VMEM((LANES, 2 * LANES), F32),

time: 150 us -> 144 us (0.960)
  the two profiles are of different devices: /device:TPU:29 before, /device:TPU:0 now
where the time goes in v4:
time: 144 us
  Pallas kernels  143 us (99%)
    pallas_call x1, Pallas kernels, on_device(): pl.pallas_call(functools.partial(gather_kernel, n_row, n_col), out_shape=...  115 us
    pallas_call x1, Pallas kernels, on_device(): pl.pallas_call(functools.partial(update_kernel, math.sqrt(rows * n_row)),...  28.2 us

profile of v4, /device:TPU:0, one launch (start us, length us, event | category | flops | bytes accessed | tf_op | source)
XLA Modules:
  0.0 144.0 jit_solution(3388108438701528058)
XLA Ops:
  0.6 115.2 %gather_and_multiply.1 = (f32[4,2048,128]{2,1,0:T(8,128)}, f32[512,2048]{1,0:T(8,128)}, f32[512,512]{1,0:T(8,128)}) custom-call(f32[2048,2048]{1,0:T(8,128)} %a_ref.1), custom_call_target="tpu_custom_call" | custom-call | tf_op jit(solution)/shard_map/gather_and_multiply/pallas_call | solution.py:529
  115.8 28.2 %factor_and_update.1 = (f32[512,2048]{1,0:T(8,128)}, f32[2048,512]{1,0:T(8,128)}, f32[2048,2048]{1,0:T(8,128)}) custom-call(f32[512,512]{1,0:T(8,128)} %get-tuple-element.6.inv_ref, f32[512,2048]{1,0:T(8,128)} %get-tuple-element.7.z_ref, f32[4,2048,128]{2,1,0:T(8,128)} %get-tuple-element.8.w_ref, f32[2048,2048]{1,0:T(8,128)} %a_ref.1), custom_call_target="tpu_custom_call" | custom-call | tf_op jit(solution)/shard_map/factor_and_update/pallas_call | solution.py:578

commit v5 on v4

--- a/solution.py
+++ b/solution.py
@@ -574,7 +574,7 @@
             collective_id=0, has_side_effects=True, vmem_limit_bytes=60 * 1024 * 1024),
         name="gather_and_multiply",
     )(matrix)
-    step = 256
+    step = 512
     return pl.pallas_call(
         functools.partial(update_kernel, math.sqrt(rows * n_row)),
         grid=(rows // step,),

time: 144 us -> 143 us (level)
  no operation moved by 1% of the time
where the time goes in v5:
time: 143 us
  Pallas kernels  142 us (99%)
    pallas_call x1, Pallas kernels, on_device(): pl.pallas_call(functools.partial(gather_kernel, n_row, n_col), out_shape=...  115 us
    pallas_call x1, Pallas kernels, on_device(): pl.pallas_call(functools.partial(update_kernel, math.sqrt(rows * n_row)),...  26.9 us

profile of v5, /device:TPU:0, one launch (start us, length us, event | category | flops | bytes accessed | tf_op | source)
XLA Modules:
  0.0 142.8 jit_solution(16754168117908927673)
XLA Ops:
  0.6 115.2 %gather_and_multiply.1 = (f32[4,2048,128]{2,1,0:T(8,128)}, f32[512,2048]{1,0:T(8,128)}, f32[512,512]{1,0:T(8,128)}) custom-call(f32[2048,2048]{1,0:T(8,128)} %a_ref.1), custom_call_target="tpu_custom_call" | custom-call | tf_op jit(solution)/shard_map/gather_and_multiply/pallas_call | solution.py:529
  115.8 26.9 %factor_and_update.1 = (f32[512,2048]{1,0:T(8,128)}, f32[2048,512]{1,0:T(8,128)}, f32[2048,2048]{1,0:T(8,128)}) custom-call(f32[512,512]{1,0:T(8,128)} %get-tuple-element.6.inv_ref, f32[512,2048]{1,0:T(8,128)} %get-tuple-element.7.z_ref, f32[4,2048,128]{2,1,0:T(8,128)} %get-tuple-element.8.w_ref, f32[2048,2048]{1,0:T(8,128)} %a_ref.1), custom_call_target="tpu_custom_call" | custom-call | tf_op jit(solution)/shard_map/factor_and_update/pallas_call | solution.py:578
